TPU v7x, 32 devices: a whole 2x2x4 slice. The times are simulated.
32 devices in a mesh: dp: 8 (over z, x), ctx: 4 (over y, core).
Axes of the slice: x: 2, y: 2, z: 4, core: 2. Of those that a mesh axis runs over, the one named last changes fastest.
Arguments:
- queries: bfloat16 [8, 4, 2, 64, 2048], P('dp', 'ctx'), may hold values from -6 to 6
- keys: bfloat16 [8, 4, 2, 64, 512], P('dp', 'ctx'), may hold values from -6 to 6
- values: bfloat16 [8, 4, 2, 64, 512], P('dp', 'ctx'), may hold values from -6 to 6
- out_grad: bfloat16 [8, 4, 2, 64, 2048], P('dp', 'ctx'), may hold values from -6 to 6
- layer_input: bfloat16 [8, 4, 2, 64, 4096], P('dp', 'ctx'), may hold values from -6 to 6
- doc_lengths: int32 [8, 16], P('dp'), may hold values from 1 to 64, as said below
Outputs:
- query_grad: bfloat16 [8, 4, 2, 64, 2048], P('dp', 'ctx')
- key_grad: bfloat16 [8, 4, 2, 64, 512], P('dp', 'ctx')
- value_grad: bfloat16 [8, 4, 2, 64, 512], P('dp', 'ctx')
- weight_grad: float32 [4096, 512], P('ctx', 'dp')
Inputs may be any that keep to these rules, and one draw needn't show every extreme that they name: `doc_lengths`: each sequence is 16 documents laid end to end that fill its 512 tokens; no document is longer than 64 tokens, and one of each sequence has exactly 64.
All inputs are finite; a program needn't handle non-finite values.
Results may differ from a plain program's by a relative error of at most 0.03.
Values may be sent and summed in bfloat16 or wider, within the bound.
A program may use at most 64 MiB of HBM per device.

v0:
```python
import math

import jax
import jax.numpy as jnp
from jax import lax
from jax.sharding import PartitionSpec as P

HD = 128


def from_behind(value, axis, steps):
    count = lax.axis_size(axis)
    first, last = (max(0, -steps), min(count, count - steps))
    return lax.ppermute(value, axis, [(source, source + steps) for source in range(first, last)])


def doc_index(starts, positions):
    return jnp.sum((starts <= positions[..., None]).astype(jnp.int32), axis=-1) - 1


def attend(query_rows, key_block, value_block, grad_rows, query_pos, key_pos, starts):
    blocks, rows, query_width = query_rows.shape
    columns = key_block.shape[1]
    kv_heads = key_block.shape[2] // HD
    groups = query_width // HD // kv_heads
    inverse_root = 1.0 / math.sqrt(HD)
    query_heads = query_rows.reshape(blocks, rows, kv_heads, groups, HD)
    grad_heads = grad_rows.reshape(blocks, rows, kv_heads, groups, HD)
    key_heads = key_block.reshape(blocks, columns, kv_heads, HD)
    value_heads = value_block.reshape(blocks, columns, kv_heads, HD)
    query_doc = doc_index(starts, query_pos)
    key_doc = doc_index(starts, key_pos)
    allowed = (
        (query_doc[:, :, None] == key_doc[:, None, :])
        & (key_pos[:, None, :] <= query_pos[:, :, None])
        & (key_pos[:, None, :] >= 0)
    )
    scores = (
        jnp.einsum("bqngd,bknd->bngqk", query_heads, key_heads, preferred_element_type=jnp.float32)
        * inverse_root
    )
    scores = jnp.where(allowed[:, None, None], scores, -1e30)
    top_score = jnp.max(scores, axis=-1, keepdims=True)
    log_total = top_score + jnp.log(jnp.sum(jnp.exp(scores - top_score), axis=-1, keepdims=True))
    probs = jnp.exp(scores - log_total)
    probs_low = probs.astype(jnp.bfloat16)
    attn_out = jnp.einsum(
        "bngqk,bknd->bqngd", probs_low, value_heads, preferred_element_type=jnp.float32
    ).astype(jnp.bfloat16)
    delta = jnp.sum(grad_heads.astype(jnp.float32) * attn_out.astype(jnp.float32), axis=-1)
    dprob = jnp.einsum(
        "bqngd,bknd->bngqk", grad_heads, value_heads, preferred_element_type=jnp.float32
    )
    dscore = (probs * (dprob - jnp.transpose(delta, (0, 2, 3, 1))[..., None])).astype(jnp.bfloat16)
    query_grad = (
        jnp.einsum("bngqk,bknd->bqngd", dscore, key_heads, preferred_element_type=jnp.float32)
        * inverse_root
    ).astype(jnp.bfloat16)
    key_terms = (
        jnp.einsum("bngqk,bqngd->bknd", dscore, query_heads, preferred_element_type=jnp.float32)
        * inverse_root
    )
    value_terms = jnp.einsum(
        "bngqk,bqngd->bknd", probs_low, grad_heads, preferred_element_type=jnp.float32
    )
    return (
        query_grad.reshape(blocks, rows, query_width),
        key_terms.reshape(blocks, columns, kv_heads * HD),
        value_terms.reshape(blocks, columns, kv_heads * HD),
    )


def body(queries, keys, values, out_grad, layer_input, doc_lengths):
    span_rows = queries.shape[3]
    query_rows = queries[0, 0]
    key_rows = keys[0, 0]
    value_rows = values[0, 0]
    grad_rows = out_grad[0, 0]
    lengths = doc_lengths[0]
    starts = jnp.cumsum(lengths) - lengths
    device_place = lax.axis_index("ctx")
    ctx_count = lax.axis_size("ctx")
    offsets = jnp.arange(span_rows, dtype=jnp.int32)
    lower_pos = device_place * span_rows + offsets
    upper_pos = (2 * ctx_count - 1 - device_place) * span_rows + offsets
    at_fold = device_place == ctx_count - 1
    arrived = []
    for direction in (1, -1):
        arrived.append(from_behind((key_rows, value_rows), "ctx", direction))
    below_keys = arrived[0][0][0]
    below_values = arrived[0][1][0]
    above_keys = arrived[1][0][1]
    above_values = arrived[1][1][1]
    upper_prev_keys = jnp.where(at_fold, key_rows[0], above_keys)
    upper_prev_values = jnp.where(at_fold, value_rows[0], above_values)
    key_block = jnp.stack(
        [
            jnp.concatenate([below_keys, key_rows[0]], axis=0),
            jnp.concatenate([upper_prev_keys, key_rows[1]], axis=0),
        ]
    )
    value_block = jnp.stack(
        [
            jnp.concatenate([below_values, value_rows[0]], axis=0),
            jnp.concatenate([upper_prev_values, value_rows[1]], axis=0),
        ]
    )
    query_pos = jnp.stack([lower_pos, upper_pos])
    key_pos = jnp.stack(
        [
            jnp.concatenate([lower_pos - span_rows, lower_pos]),
            jnp.concatenate([upper_pos - span_rows, upper_pos]),
        ]
    )
    query_grad, key_terms, value_terms = attend(
        query_rows, key_block, value_block, grad_rows, query_pos, key_pos, starts
    )
    lower_keys = key_terms[0, span_rows:] + jnp.where(at_fold, key_terms[1, :span_rows], 0.0)
    lower_values = value_terms[0, span_rows:] + jnp.where(at_fold, value_terms[1, :span_rows], 0.0)
    upper_keys = key_terms[1, span_rows:]
    upper_values = value_terms[1, span_rows:]
    down_keys = key_terms[0, :span_rows]
    down_values = value_terms[0, :span_rows]
    up_keys = jnp.where(at_fold, 0.0, key_terms[1, :span_rows])
    up_values = jnp.where(at_fold, 0.0, value_terms[1, :span_rows])
    blank = jnp.zeros_like(down_keys)
    key_total = jnp.stack([lower_keys, upper_keys])
    value_total = jnp.stack([lower_values, upper_values])
    for direction, sent_keys, sent_values in (
        (-1, jnp.stack([down_keys, blank]), jnp.stack([down_values, blank])),
        (1, jnp.stack([blank, up_keys]), jnp.stack([blank, up_values])),
    ):
        came_keys, came_values = (
            from_behind(sent_keys.astype(jnp.bfloat16), "ctx", direction).astype(sent_keys.dtype),
            from_behind(sent_values.astype(jnp.bfloat16), "ctx", direction).astype(
                sent_values.dtype
            ),
        )
        key_total = key_total + came_keys
        value_total = value_total + came_values
    key_grad = key_total.astype(jnp.bfloat16)
    value_grad = value_total.astype(jnp.bfloat16)
    input_rows = layer_input[0, 0].reshape(2 * span_rows, layer_input.shape[4])
    grad_values = value_grad.reshape(2 * span_rows, value_grad.shape[2])
    row_block = lax.psum_scatter(
        lax.dot_general(
            input_rows, grad_values, (((0,), (0,)), ((), ())), preferred_element_type=jnp.float32
        ).astype(jnp.bfloat16),
        "ctx",
        scatter_dimension=0,
        tiled=True,
    ).astype(jnp.float32)
    weight_grad = lax.psum_scatter(row_block, "dp", scatter_dimension=1, tiled=True) / jnp.float32(
        lax.axis_size("dp")
    )
    return (query_grad[None, None], key_grad[None, None], value_grad[None, None], weight_grad)


def solution(mesh):
    in_specs = (
        P("dp", "ctx", None, None, None),
        P("dp", "ctx", None, None, None),
        P("dp", "ctx", None, None, None),
        P("dp", "ctx", None, None, None),
        P("dp", "ctx", None, None, None),
        P("dp", None),
    )
    out_specs = (
        P("dp", "ctx", None, None, None),
        P("dp", "ctx", None, None, None),
        P("dp", "ctx", None, None, None),
        P("ctx", "dp"),
    )
    return jax.shard_map(body, mesh=mesh, in_specs=in_specs, out_specs=out_specs, check_vma=False)
```

profile of v0, /device:TPU:0, one launch (start us, length us, event | category | flops | bytes accessed | tf_op | source)
XLA Modules:
  0.0 169.0 jit_solution(11205780539111671788)
XLA Ops:
  7.2 0.0 copy-start
  7.2 0.0 reduce-scatter.3.cloned.1.call-start
  7.2 1.4 collective-permute-start.1
  8.7 3.0 %collective-permute-start = (bf16[2,64,512]{2,1,0:T(8,128)(2,1)}, bf16[2,64,512]{2,1,0:T(8,128)(2,1)S(1)}, u32[]{:S(2)}, u32[]{:S(2)}) collective-permute-start(bf16[2,64,512]{2,1,0:T(8,128)(2,1)} %bitcast.112), channel_id=1, source_target_pairs={{0,1},{1,2},{2,3},{4,5},{5,6},{6,7},{8,9},{9,10},{10,11},{12,13},{... | collective-permute-start | bytes 393224 | tf_op jit(solution)/shard_map/ppermute | solution.py:14
  11.8 0.1 add_bitcast_fusion
  11.8 0.1 add_bitcast_fusion.1
  11.9 0.9 fusion.33
  12.8 0.7 copy.51
  13.6 0.1 reduce
  13.7 0.7 bitcast_subtract_fusion
  14.4 0.1 convert_reduce_fusion
  14.5 0.1 convert_reduce_fusion.1
  14.7 1.4 reshape_squeeze.10
  16.1 1.4 reshape_squeeze.9
  17.5 0.1 and_and_fusion
  17.6 0.0 collective-permute-done
  17.7 0.5 fusion.36
  18.3 0.7 exponential_reduce_fusion
  19.0 0.9 fusion.16
  19.9 0.9 fusion.30
  20.8 0.7 copy.82
  21.6 1.5 stack.56
  23.1 1.3 collective-permute-start.6
  24.4 1.1 copy.80
  25.4 0.7 stack.57
  26.1 1.7 %copy.81 = f32[1,64,512]{2,1,0:T(8,128)} copy(f32[1,64,512]{1,2,0:T(8,128)} %get-tuple-element.5) | data formatting | bytes 262144
  27.8 0.8 copy.79
  28.6 5.1 %collective-permute-start.7 = (bf16[2,64,512]{2,1,0:T(8,128)(2,1)}, bf16[2,64,512]{2,1,0:T(8,128)(2,1)S(1)}, u32[]{:S(2)}, u32[]{:S(2)}) collective-permute-start(bf16[2,64,512]{2,1,0:T(8,128)(2,1)} %stack.57), channel_id=1, source_target_pairs={{0,1},{1,2},{2,3},{4,5},{5,6},{6,7},{8,9},{9,10},{10,11},{12,13},{... | collective-permute-start | bytes 393224 | tf_op jit(solution)/shard_map/ppermute | solution.py:14
  33.7 0.9 select_add_fusion
  34.7 0.0 collective-permute-done.6
  34.7 0.2 collective-permute-done.7
  34.9 1.0 fusion.22
  35.9 0.0 copy-start.1
  35.9 3.2 %fusion = bf16[4096,512]{0,1:T(8,128)(2,1)} fusion(bf16[128,512]{1,0:T(8,128)(2,1)S(1)} %bitcast.109, bf16[128,4096]{1,0:T(8,128)(2,1)S(1)} %bitcast.104), kind=kOutput, calls=%fused_computation.1 | convolution fusion | flops 538968064 | bytes 5373952 | tf_op jit(solution)/shard_map/dot_general | solution.py:146
  39.2 0.0 reduce-scatter.3.cloned.1.call-update
  39.2 0.0 reduce-scatter.5.cloned.1.call-start
  39.2 49.4 %reduce-scatter.3.cloned.1.call-done = bf16[1024,512]{0,1:T(8,128)(2,1)} async-done(((bf16[4096,512]{0,1:T(8,128)(2,1)}), bf16[1024,512]{0,1:T(8,128)(2,1)}) %reduce-scatter.3.cloned.1.call-update) | async-done | bytes 1048592 | tf_op jit(solution)/shard_map/reduce_scatter | solution.py:145
  88.6 2.8 %convert_element_type.80 = f32[1024,512]{0,1:T(8,128)} convert(bf16[1024,512]{0,1:T(8,128)(2,1)} %reduce-scatter.3.cloned.1.call-done) | non-fusion elementwise | flops 524288 | bytes 3145728 | tf_op jit(solution)/shard_map/convert_element_type | solution.py:152
  91.4 0.0 reduce-scatter.5.cloned.1.call-update
  91.5 1.3 collective-permute-start.3
  92.8 3.7 %collective-permute-start.2 = (bf16[2,64,512]{2,1,0:T(8,128)(2,1)S(1)}, bf16[2,64,512]{2,1,0:T(8,128)(2,1)}, u32[]{:S(2)}, u32[]{:S(2)}) collective-permute-start(bf16[2,64,512]{2,1,0:T(8,128)(2,1)S(1)} %bitcast.114), channel_id=1, source_target_pairs={{0,1},{1,2},{2,3},{4,5},{5,6},{6,7},{8,9},{9,10},{10,11},{12,13},{... | collective-permute-start | bytes 393224 | tf_op jit(solution)/shard_map/ppermute | solution.py:14
  96.6 0.3 collective-permute-done.2
  96.9 0.9 copy_bitcast_fusion
  97.8 0.0 collective-permute-done.3
  97.8 0.9 fusion.34
  98.6 0.6 fusion.10
  99.3 0.8 fusion.5
  100.1 0.8 copy-done.2
  100.9 0.3 fusion.11
  101.2 0.4 copy.60
  101.6 1.2 broadcast_in_dim_reshape.3
  102.8 1.4 fusion.12
  104.2 0.1 copy.78
  104.3 1.3 collective-permute-start.4
  105.6 0.2 fusion.31
  105.8 0.1 copy.75
  105.9 0.1 copy.76
  106.1 0.1 copy.77
  106.2 4.5 %collective-permute-start.5 = (bf16[2,64,512]{2,1,0:T(8,128)(2,1)S(1)}, bf16[2,64,512]{2,1,0:T(8,128)(2,1)S(1)}, u32[]{:S(2)}, u32[]{:S(2)}) collective-permute-start(bf16[2,64,512]{2,1,0:T(8,128)(2,1)S(1)} %stack.54), channel_id=1, source_target_pairs={{0,1},{1,2},{2,3},{4,5},{5,6},{6,7},{8,9},{9,10},{10,11},{12,13},{... | collective-permute-start | bytes 393224 | tf_op jit(solution)/shard_map/ppermute | solution.py:14
  110.7 0.0 collective-permute-done.4
  110.7 0.9 collective-permute-done.5
  111.6 0.7 fusion.23
  112.3 48.1 %reduce-scatter.5.cloned.1.call-done = f32[1024,64]{0,1:T(8,128)} async-done(((f32[1024,512]{0,1:T(8,128)}), f32[1024,64]{0,1:T(8,128)}) %reduce-scatter.5.cloned.1.call-update) | async-done | bytes 262160 | tf_op jit(solution)/shard_map/reduce_scatter | solution.py:153
  160.5 1.7 broadcast_multiply_fusion
  (48 shorter events, 0.4 us)
Async XLA Ops:
  7.2 28.8 %copy-start = (bf16[1,1,2,64,4096]{4,3,2,1,0:T(8,128)(2,1)S(1)}, bf16[1,1,2,64,4096]{4,3,2,1,0:T(8,128)(2,1)}, u32[]{:S(2)}) copy-start(bf16[1,1,2,64,4096]{4,3,2,1,0:T(8,128)(2,1)} %param.10) | copy-start | bytes 3145732
  7.2 81.4 %reduce-scatter.3.cloned.1.call-start = ((), (), s32[]{:S(2)}) async-start(), calls=%async_computation.2 | async-start | bytes 5242880 | tf_op jit(solution)/shard_map/reduce_scatter | solution.py:145
  7.2 10.4 %collective-permute-start.1 = (bf16[2,64,512]{2,1,0:T(8,128)(2,1)}, bf16[2,64,512]{2,1,0:T(8,128)(2,1)S(1)}, u32[]{:S(2)}, u32[]{:S(2)}) collective-permute-start(bf16[2,64,512]{2,1,0:T(8,128)(2,1)} %bitcast.111), channel_id=1, source_target_pairs={{1,0},{2,1},{3,2},{5,4},{6,5},{7,6},{9,8},{10,9},{11,10},{13,12},{... | collective-permute-start | bytes 393224 | tf_op jit(solution)/shard_map/ppermute | solution.py:14
  8.7 8.9 %collective-permute-start = (bf16[2,64,512]{2,1,0:T(8,128)(2,1)}, bf16[2,64,512]{2,1,0:T(8,128)(2,1)S(1)}, u32[]{:S(2)}, u32[]{:S(2)}) collective-permute-start(bf16[2,64,512]{2,1,0:T(8,128)(2,1)} %bitcast.112), channel_id=1, source_target_pairs={{0,1},{1,2},{2,3},{4,5},{5,6},{6,7},{8,9},{9,10},{10,11},{12,13},{... | collective-permute-start | bytes 393224 | tf_op jit(solution)/shard_map/ppermute | solution.py:14
  14.6 3.6 %copy-start.4 = (bf16[1,64,4,128]{3,1,2,0:T(8,128)(2,1)}, bf16[1,64,4,128]{3,1,2,0:T(8,128)(2,1)S(1)}, u32[]{:S(2)}) copy-start(bf16[1,64,4,128]{3,1,2,0:T(8,128)(2,1)S(1)} %copy.50) | copy-start | bytes 196612
  17.6 1.3 copy-start.6
  17.7 1.3 copy-start.8
  17.7 1.3 copy-start.10
  23.1 11.6 %collective-permute-start.6 = (bf16[2,64,512]{2,1,0:T(8,128)(2,1)}, bf16[2,64,512]{2,1,0:T(8,128)(2,1)}, u32[]{:S(2)}, u32[]{:S(2)}) collective-permute-start(bf16[2,64,512]{2,1,0:T(8,128)(2,1)} %stack.56), channel_id=1, source_target_pairs={{1,0},{2,1},{3,2},{5,4},{6,5},{7,6},{9,8},{10,9},{11,10},{13,12},{... | collective-permute-start | bytes 393224 | tf_op jit(solution)/shard_map/ppermute | solution.py:14
  28.6 6.3 %collective-permute-start.7 = (bf16[2,64,512]{2,1,0:T(8,128)(2,1)}, bf16[2,64,512]{2,1,0:T(8,128)(2,1)S(1)}, u32[]{:S(2)}, u32[]{:S(2)}) collective-permute-start(bf16[2,64,512]{2,1,0:T(8,128)(2,1)} %stack.57), channel_id=1, source_target_pairs={{0,1},{1,2},{2,3},{4,5},{5,6},{6,7},{8,9},{9,10},{10,11},{12,13},{... | collective-permute-start | bytes 393224 | tf_op jit(solution)/shard_map/ppermute | solution.py:14
  35.9 3.3 %copy-start.1 = (bf16[2,64,512]{2,1,0:T(8,128)(2,1)}, bf16[2,64,512]{2,1,0:T(8,128)(2,1)S(1)}, u32[]{:S(2)}) copy-start(bf16[2,64,512]{2,1,0:T(8,128)(2,1)S(1)} %fusion.22) | copy-start | bytes 393220
  39.2 52.3 %copy-start.3 = (bf16[1,1,2,64,512]{4,3,2,1,0:T(8,128)(2,1)S(1)}, bf16[1,1,2,64,512]{4,3,2,1,0:T(8,128)(2,1)}, u32[]{:S(2)}) copy-start(bf16[1,1,2,64,512]{4,3,2,1,0:T(8,128)(2,1)} %param.8) | copy-start | bytes 393220
  39.2 121.3 %reduce-scatter.5.cloned.1.call-start = ((), (), s32[]{:S(2)}) async-start(), calls=%async_computation.3 | async-start | bytes 2359296 | tf_op jit(solution)/shard_map/reduce_scatter | solution.py:153
  91.4 9.4 %copy-start.5 = (bf16[1,64,4,128]{3,1,2,0:T(8,128)(2,1)S(1)}, bf16[1,64,4,128]{3,1,2,0:T(8,128)(2,1)}, u32[]{:S(2)}) copy-start(bf16[1,64,4,128]{3,1,2,0:T(8,128)(2,1)} %copy-done.4) | copy-start | bytes 196612
  91.5 6.3 %collective-permute-start.3 = (bf16[2,64,512]{2,1,0:T(8,128)(2,1)S(1)}, bf16[2,64,512]{2,1,0:T(8,128)(2,1)}, u32[]{:S(2)}, u32[]{:S(2)}) collective-permute-start(bf16[2,64,512]{2,1,0:T(8,128)(2,1)S(1)} %bitcast.113), channel_id=1, source_target_pairs={{1,0},{2,1},{3,2},{5,4},{6,5},{7,6},{9,8},{10,9},{11,10},{13,12},{... | collective-permute-start | bytes 393224 | tf_op jit(solution)/shard_map/ppermute | solution.py:14
  92.8 4.1 %collective-permute-start.2 = (bf16[2,64,512]{2,1,0:T(8,128)(2,1)S(1)}, bf16[2,64,512]{2,1,0:T(8,128)(2,1)}, u32[]{:S(2)}, u32[]{:S(2)}) collective-permute-start(bf16[2,64,512]{2,1,0:T(8,128)(2,1)S(1)} %bitcast.114), channel_id=1, source_target_pairs={{0,1},{1,2},{2,3},{4,5},{5,6},{6,7},{8,9},{9,10},{10,11},{12,13},{... | collective-permute-start | bytes 393224 | tf_op jit(solution)/shard_map/ppermute | solution.py:14
  96.5 4.4 %copy-start.7 = (bf16[1,64,4,128]{3,1,2,0:T(8,128)(2,1)S(1)}, bf16[1,64,4,128]{3,1,2,0:T(8,128)(2,1)}, u32[]{:S(2)}) copy-start(bf16[1,64,4,128]{3,1,2,0:T(8,128)(2,1)} %copy-done.6) | copy-start | bytes 196612
  96.5 4.4 %copy-start.9 = (bf16[1,64,4,128]{3,1,2,0:T(8,128)(2,1)S(1)}, bf16[1,64,4,128]{3,1,2,0:T(8,128)(2,1)}, u32[]{:S(2)}) copy-start(bf16[1,64,4,128]{3,1,2,0:T(8,128)(2,1)} %copy-done.8) | copy-start | bytes 196612
  96.5 4.3 %copy-start.11 = (bf16[1,64,4,128]{3,1,2,0:T(8,128)(2,1)S(1)}, bf16[1,64,4,128]{3,1,2,0:T(8,128)(2,1)}, u32[]{:S(2)}) copy-start(bf16[1,64,4,128]{3,1,2,0:T(8,128)(2,1)} %copy-done.10) | copy-start | bytes 196612
  100.1 0.8 copy-start.2
  104.3 6.4 %collective-permute-start.4 = (bf16[2,64,512]{2,1,0:T(8,128)(2,1)S(1)}, bf16[2,64,512]{2,1,0:T(8,128)(2,1)S(1)}, u32[]{:S(2)}, u32[]{:S(2)}) collective-permute-start(bf16[2,64,512]{2,1,0:T(8,128)(2,1)S(1)} %stack.53), channel_id=1, source_target_pairs={{1,0},{2,1},{3,2},{5,4},{6,5},{7,6},{9,8},{10,9},{11,10},{13,12},{... | collective-permute-start | bytes 393224 | tf_op jit(solution)/shard_map/ppermute | solution.py:14
  106.2 5.4 %collective-permute-start.5 = (bf16[2,64,512]{2,1,0:T(8,128)(2,1)S(1)}, bf16[2,64,512]{2,1,0:T(8,128)(2,1)S(1)}, u32[]{:S(2)}, u32[]{:S(2)}) collective-permute-start(bf16[2,64,512]{2,1,0:T(8,128)(2,1)S(1)} %stack.54), channel_id=1, source_target_pairs={{0,1},{1,2},{2,3},{4,5},{5,6},{6,7},{8,9},{9,10},{10,11},{12,13},{... | collective-permute-start | bytes 393224 | tf_op jit(solution)/shard_map/ppermute | solution.py:14
Sparse Core Ops, SparseCore 0:
  39.3 49.2 reduce-scatter.2
  92.6 67.8 reduce-scatter.4
where the time goes:
time: 170 us; the launch traced here: 169 us
  waiting for transfers between devices  99 us (58%)
  starting transfers between devices  21.7 us (13%)
  local copies, waits for them, and re-layouts  15.9 us (9%)
  between operations  14.5 us (9%)
  other arithmetic  10.1 us (6%)
  matrix products  7.78 us (5%)
    reduce_scatter x1, waiting for transfers between devices, body(): lax.psum_scatter(lax.dot_general(input_rows, grad_values, (((0,), (0,)),...  49.4 us
    reduce_scatter x1, waiting for transfers between devices, body(): lax.psum_scatter(row_block, 'dp', scatter_dimension=1, tiled=True)  48.1 us
    ppermute x8, starting transfers between devices, from_behind(): lax.ppermute(value, axis, [(source, source + steps) for source in range(f...  21.6 us
    unnamed x32, local copies, waits for them, and re-layouts  5.57 us
  transfers between devices with their start and end apart: 10, of which 5 were waited for; matrix products, arithmetic and copies ran while one was open for 11% of the time, Pallas kernels for 0%

commit v1 on v0

v1 whole, which is shorter than its diff:
```python
import functools
import math

import jax
import jax.numpy as jnp
from jax import lax
from jax.experimental import pallas as pl
from jax.experimental.pallas import tpu as pltpu
from jax.sharding import PartitionSpec as P

HD = 128
MESH = pl.DeviceIdType.MESH


def dot(a, b, ca, cb):
    return lax.dot_general(a, b, (((ca,), (cb,)), ((), ())), preferred_element_type=jnp.float32)


def kernel(
    n_ctx, n_hi, n_lo, span, kvh, groups,
    q_ref, k_ref, v_ref, g_ref, li_ref, len_ref,
    dq_ref, dk_ref, dv_ref, w_ref,
    halo, sent, back, own, li_buf, vg_buf, part, recv_lo, part_hi, recv_hi, mine,
    halo_ss, halo_rs, back_ss, back_rs, li_ss, li_rs, li_own, vg_ss, vg_rs,
    lo_ss, lo_rs, hi_ss, hi_rs,
):
    me = lax.axis_index("ctx")
    place = lax.axis_index("dp")
    my_hi = place // n_lo
    my_lo = place % n_lo
    last = n_ctx - 1
    tokens = 2 * span
    chunk = li_buf.shape[1]
    blk = part.shape[2]
    inverse_root = 1.0 / math.sqrt(HD)

    def ctx_id(i):
        return (place, i)

    def dp_id(d):
        return (d, me)

    ctx_peers = [lax.rem(me + j, n_ctx) for j in range(1, n_ctx)]
    lo_peers = [lax.rem(my_lo + j, n_lo) for j in range(1, n_lo)]
    hi_peers = [lax.rem(my_hi + j, n_hi) for j in range(1, n_hi)]

    barrier = pltpu.get_barrier_semaphore()
    for peer in ctx_peers:
        pl.semaphore_signal(barrier, inc=1, device_id=ctx_id(peer), device_id_type=MESH)
    for peer in lo_peers:
        pl.semaphore_signal(barrier, inc=1, device_id=dp_id(my_hi * n_lo + peer), device_id_type=MESH)
    for peer in hi_peers:
        pl.semaphore_signal(barrier, inc=1, device_id=dp_id(peer * n_lo + my_lo), device_id_type=MESH)
    pl.semaphore_wait(barrier, n_ctx + n_lo + n_hi - 3)

    def halo_copy(slot, which):
        source = (k_ref, v_ref)[which]
        return pltpu.make_async_remote_copy(
            src_ref=source.at[pl.ds(slot * span, span)],
            dst_ref=halo.at[slot, which],
            send_sem=halo_ss.at[slot, which],
            recv_sem=halo_rs.at[slot, which],
            device_id=ctx_id(jnp.minimum(me + 1, last) if slot == 0 else jnp.maximum(me - 1, 0)),
            device_id_type=MESH,
        )

    def back_copy(slot):
        return pltpu.make_async_remote_copy(
            src_ref=sent.at[slot],
            dst_ref=back.at[slot],
            send_sem=back_ss.at[slot],
            recv_sem=back_rs.at[slot],
            device_id=ctx_id(jnp.maximum(me - 1, 0) if slot == 0 else jnp.minimum(me + 1, last)),
            device_id_type=MESH,
        )

    @pl.when(me < last)
    def _():
        for which in range(2):
            halo_copy(0, which).start()

    @pl.when(me > 0)
    def _():
        for which in range(2):
            halo_copy(1, which).start()

    def li_copy(j):
        peer = ctx_peers[j]
        return pltpu.make_async_remote_copy(
            src_ref=li_ref.at[:, pl.ds(pl.multiple_of(peer * chunk, chunk), chunk)],
            dst_ref=li_buf.at[pl.ds(pl.multiple_of(me * tokens, tokens), tokens)],
            send_sem=li_ss.at[j],
            recv_sem=li_rs.at[j],
            device_id=ctx_id(peer),
            device_id_type=MESH,
        )

    li_local = pltpu.make_async_copy(
        li_ref.at[:, pl.ds(pl.multiple_of(me * chunk, chunk), chunk)],
        li_buf.at[pl.ds(pl.multiple_of(me * tokens, tokens), tokens)],
        li_own,
    )
    li_local.start()
    for j in range(n_ctx - 1):
        li_copy(j).start()

    @pl.when(me == 0)
    def _():
        halo[0] = jnp.zeros(halo.shape[1:], halo.dtype)
        back[1] = jnp.zeros(back.shape[1:], back.dtype)

    @pl.when(me == last)
    def _():
        halo[1, 0] = k_ref[pl.ds(0, span)]
        halo[1, 1] = v_ref[pl.ds(0, span)]

    for slot in range(2):
        stretch = me if slot == 0 else 2 * n_ctx - 1 - me
        first = stretch * span
        lane = lax.broadcasted_iota(jnp.int32, (1, groups * span), 1)
        pos = first + lax.rem(lane, span)
        begin = jnp.zeros_like(pos)
        run = jnp.int32(0)
        for j in range(len_ref.shape[1]):
            begin = jnp.where(pos >= run, run, begin)
            run = run + len_ref[0, j]
        key_pos = first - span + lax.broadcasted_iota(jnp.int32, (2 * span, groups * span), 0)
        allowed = (key_pos >= begin) & (key_pos <= pos)

        @pl.when((me > 0) if slot == 0 else (me < last))
        def _():
            for which in range(2):
                halo_copy(slot, which).wait_recv()

        rows = pl.ds(slot * span, span)
        for g in range(kvh):
            col = slice(g * HD, (g + 1) * HD)
            heads = [slice(h * HD, (h + 1) * HD) for h in range(g * groups, (g + 1) * groups)]
            kk = jnp.concatenate([halo[slot, 0, :, col], k_ref[rows, col]], axis=0)
            vv = jnp.concatenate([halo[slot, 1, :, col], v_ref[rows, col]], axis=0)
            qq = jnp.concatenate([q_ref[rows, h] for h in heads], axis=0)
            gg = jnp.concatenate([g_ref[rows, h] for h in heads], axis=0)
            scores = jnp.where(allowed, dot(kk, qq, 1, 1) * inverse_root, -1e30)
            weights = jnp.exp(scores - jnp.max(scores, axis=0, keepdims=True))
            probs = weights / jnp.sum(weights, axis=0, keepdims=True)
            low = probs.astype(jnp.bfloat16)
            dprob = dot(vv, gg, 1, 1)
            delta = jnp.sum(low.astype(jnp.float32) * dprob, axis=0, keepdims=True)
            ds = (probs * (dprob - delta)).astype(jnp.bfloat16)
            dk = dot(ds, qq, 1, 0) * inverse_root
            dv = dot(low, gg, 1, 0)
            dq = (dot(ds, kk, 0, 0) * inverse_root).astype(jnp.bfloat16)
            for n, h in enumerate(heads):
                dq_ref[rows, h] = dq[n * span : (n + 1) * span]
            sent[slot, 0, :, col] = dk[:span].astype(jnp.bfloat16)
            sent[slot, 1, :, col] = dv[:span].astype(jnp.bfloat16)
            own[slot, 0, :, col] = dk[span:]
            own[slot, 1, :, col] = dv[span:]

        @pl.when((me > 0) if slot == 0 else (me < last))
        def _():
            back_copy(slot).start()

    @pl.when(me == last)
    def _():
        back[0] = sent[1]

    my_rows = pl.ds(pl.multiple_of(me * tokens, tokens), tokens)
    for slot in range(2):
        @pl.when((me < last) if slot == 0 else (me > 0))
        def _():
            back_copy(slot).wait_recv()

        rows = pl.ds(slot * span, span)
        dv_ref[rows] = (own[slot, 1] + back[slot, 1].astype(jnp.float32)).astype(jnp.bfloat16)

    def vg_copy(j):
        return pltpu.make_async_remote_copy(
            src_ref=dv_ref,
            dst_ref=vg_buf.at[my_rows],
            send_sem=vg_ss.at[j],
            recv_sem=vg_rs.at[j],
            device_id=ctx_id(ctx_peers[j]),
            device_id_type=MESH,
        )

    for j in range(n_ctx - 1):
        vg_copy(j).start()
    vg_buf[my_rows] = dv_ref[...]
    for slot in range(2):
        rows = pl.ds(slot * span, span)
        dk_ref[rows] = (own[slot, 0] + back[slot, 0].astype(jnp.float32)).astype(jnp.bfloat16)
    li_local.wait()
    for j in range(n_ctx - 1):
        li_copy(j).wait_recv()
    for j in range(n_ctx - 1):
        vg_copy(j).wait_recv()

    def lo_copy(h, j):
        peer = lo_peers[j]
        return pltpu.make_async_remote_copy(
            src_ref=part.at[peer, h],
            dst_ref=recv_lo.at[j, h],
            send_sem=lo_ss.at[j, h],
            recv_sem=lo_rs.at[j, h],
            device_id=dp_id(my_hi * n_lo + peer),
            device_id_type=MESH,
        )

    wide = n_lo * blk
    for h in range(n_hi):
        product = dot(vg_buf[:, h * wide : (h + 1) * wide], li_buf[...], 0, 0)
        for l in range(n_lo):
            part[l, h] = product[l * blk : (l + 1) * blk].astype(jnp.bfloat16)
        for j in range(n_lo - 1):
            lo_copy(h, j).start()

    def hi_send(h):
        return pltpu.make_async_remote_copy(
            src_ref=part_hi.at[h],
            dst_ref=recv_hi.at[lax.rem(my_hi - h + n_hi, n_hi)],
            send_sem=hi_ss.at[h],
            recv_sem=hi_rs.at[lax.rem(my_hi - h + n_hi, n_hi)],
            device_id=dp_id(h * n_lo + my_lo),
            device_id_type=MESH,
        )

    for h in range(n_hi):
        for j in range(n_lo - 1):
            lo_copy(h, j).wait_recv()
        total = part[my_lo, h].astype(jnp.float32)
        for j in range(n_lo - 1):
            total = total + recv_lo[j, h].astype(jnp.float32)

        @pl.when(my_hi == h)
        def _():
            mine[...] = total

        @pl.when(my_hi != h)
        def _():
            part_hi[h] = total.astype(jnp.bfloat16)
            hi_send(h).start()

    def hi_recv(d):
        return pltpu.make_async_remote_copy(
            src_ref=part_hi.at[0],
            dst_ref=recv_hi.at[d],
            send_sem=hi_ss.at[0],
            recv_sem=hi_rs.at[d],
            device_id=dp_id(hi_peers[d - 1] * n_lo + my_lo),
            device_id_type=MESH,
        )

    for d in range(1, n_hi):
        hi_recv(d).wait_recv()
    total = mine[...]
    for d in range(1, n_hi):
        total = total + recv_hi[d].astype(jnp.float32)
    w_ref[...] = total * (1.0 / (n_hi * n_lo))

    @pl.when(me < last)
    def _():
        for which in range(2):
            halo_copy(0, which).wait_send()
        back_copy(1).wait_send()

    @pl.when(me > 0)
    def _():
        for which in range(2):
            halo_copy(1, which).wait_send()
        back_copy(0).wait_send()

    for j in range(n_ctx - 1):
        li_copy(j).wait_send()
        vg_copy(j).wait_send()
    for h in range(n_hi):
        for j in range(n_lo - 1):
            lo_copy(h, j).wait_send()

        @pl.when(my_hi != h)
        def _():
            hi_send(h).wait_send()


def body(n_ctx, n_dp, queries, keys, values, out_grad, layer_input, doc_lengths):
    span = queries.shape[3]
    tokens = 2 * span
    q = queries.reshape(tokens, queries.shape[4])
    k = keys.reshape(tokens, keys.shape[4])
    v = values.reshape(tokens, values.shape[4])
    g = out_grad.reshape(tokens, out_grad.shape[4])
    li = layer_input.reshape(tokens, layer_input.shape[4])
    kv_width = k.shape[1]
    kvh = kv_width // HD
    groups = q.shape[1] // kv_width
    chunk = li.shape[1] // n_ctx
    blk = kv_width // n_dp
    n_lo = 2 ** ((n_dp.bit_length() - 1) // 2)
    n_hi = n_dp // n_lo
    bf16, f32 = jnp.bfloat16, jnp.float32
    dma = pltpu.SemaphoreType.DMA
    vmem = pl.BlockSpec(memory_space=pltpu.VMEM)
    outs = pl.pallas_call(
        functools.partial(kernel, n_ctx, n_hi, n_lo, span, kvh, groups),
        out_shape=(
            jax.ShapeDtypeStruct(q.shape, bf16),
            jax.ShapeDtypeStruct(k.shape, bf16),
            jax.ShapeDtypeStruct(v.shape, bf16),
            jax.ShapeDtypeStruct((blk, chunk), f32),
        ),
        in_specs=[vmem, vmem, vmem, vmem, pl.BlockSpec(memory_space=pl.ANY),
                  pl.BlockSpec(memory_space=pltpu.SMEM)],
        out_specs=(vmem, vmem, vmem, vmem),
        scratch_shapes=[
            pltpu.VMEM((2, 2, span, kv_width), bf16),
            pltpu.VMEM((2, 2, span, kv_width), bf16),
            pltpu.VMEM((2, 2, span, kv_width), bf16),
            pltpu.VMEM((2, 2, span, kv_width), f32),
            pltpu.VMEM((n_ctx * tokens, chunk), bf16),
            pltpu.VMEM((n_ctx * tokens, kv_width), bf16),
            pltpu.VMEM((n_lo, n_hi, blk, chunk), bf16),
            pltpu.VMEM((n_lo - 1, n_hi, blk, chunk), bf16),
            pltpu.VMEM((n_hi, blk, chunk), bf16),
            pltpu.VMEM((n_hi, blk, chunk), bf16),
            pltpu.VMEM((blk, chunk), f32),
            dma((2, 2)), dma((2, 2)), dma((2,)), dma((2,)),
            dma((n_ctx - 1,)), dma((n_ctx - 1,)), dma,
            dma((n_ctx - 1,)), dma((n_ctx - 1,)),
            dma((n_lo - 1, n_hi)), dma((n_lo - 1, n_hi)), dma((n_hi,)), dma((n_hi,)),
        ],
        compiler_params=pltpu.CompilerParams(
            collective_id=0, has_side_effects=True, vmem_limit_bytes=40 * 1024 * 1024
        ),
        name="attention_grads",
    )(q, k, v, g, li, doc_lengths)
    dq, dk, dv, w = outs
    return (
        dq.reshape(queries.shape),
        dk.reshape(keys.shape),
        dv.reshape(values.shape),
        w.T,
    )


def solution(mesh):
    tokens = P("dp", "ctx", None, None, None)
    return jax.shard_map(
        functools.partial(body, mesh.shape["ctx"], mesh.shape["dp"]),
        mesh=mesh,
        in_specs=(tokens, tokens, tokens, tokens, tokens, P("dp", None)),
        out_specs=(tokens, tokens, tokens, P("ctx", "dp")),
        check_vma=False,
    )
```

time: 170 us -> 59.1 us (0.35)
  the two profiles are of different devices: /device:TPU:0 before, /device:TPU:29 now
where the time goes in v1:
time: 59.1 us; the launch traced here: 58.8 us
  Pallas kernels  49.6 us (84%)
  local copies, waits for them, and re-layouts  8.57 us (15%)
  between operations  0.66 us (1%)
    pallas_call x1, Pallas kernels, body(): pl.pallas_call(functools.partial(kernel, n_ctx, n_hi, n_lo, span, kvh, gr...  49.6 us
    unnamed x16, local copies, waits for them, and re-layouts  8.57 us

profile of v1, /device:TPU:29, one launch (start us, length us, event | category | flops | bytes accessed | tf_op | source)
XLA Modules:
  0.0 58.8 jit_solution(8199358037577343730)
XLA Ops:
  0.6 0.0 copy-start.5
  0.6 0.6 %copy-done.5 = s32[1,16]{1,0:T(1,128)S(1)} copy-done((s32[1,16]{1,0:T(1,128)S(1)}, s32[1,16]{1,0:T(1,128)}, u32[]{:S(2)}) %copy-start.5) | copy-done | bytes 88
  1.3 0.0 copy-start
  1.3 1.2 %copy-done = bf16[1,1,2,64,4096]{4,3,2,1,0:T(8,128)(2,1)S(1)} copy-done((bf16[1,1,2,64,4096]{4,3,2,1,0:T(8,128)(2,1)S(1)}, bf16[1,1,2,64,4096]{4,3,2,1,0:T(8,128)(2,1)}, u32[]{:S(2)}) %copy-start) | copy-done | bytes 1048600
  2.5 0.0 copy-start.1
  2.5 1.0 %copy-done.1 = bf16[1,1,2,64,2048]{4,3,2,1,0:T(8,128)(2,1)S(1)} copy-done((bf16[1,1,2,64,2048]{4,3,2,1,0:T(8,128)(2,1)S(1)}, bf16[1,1,2,64,2048]{4,3,2,1,0:T(8,128)(2,1)}, u32[]{:S(2)}) %copy-start.1) | copy-done | bytes 524312
  3.6 0.0 copy-start.2
  3.6 1.0 %copy-done.2 = bf16[1,1,2,64,2048]{4,3,2,1,0:T(8,128)(2,1)S(1)} copy-done((bf16[1,1,2,64,2048]{4,3,2,1,0:T(8,128)(2,1)S(1)}, bf16[1,1,2,64,2048]{4,3,2,1,0:T(8,128)(2,1)}, u32[]{:S(2)}) %copy-start.2) | copy-done | bytes 524312
  4.6 0.0 copy-start.3
  4.6 0.9 %copy-done.3 = bf16[1,1,2,64,512]{4,3,2,1,0:T(8,128)(2,1)S(1)} copy-done((bf16[1,1,2,64,512]{4,3,2,1,0:T(8,128)(2,1)S(1)}, bf16[1,1,2,64,512]{4,3,2,1,0:T(8,128)(2,1)}, u32[]{:S(2)}) %copy-start.3) | copy-done | bytes 131096
  5.5 0.0 copy-start.4
  5.5 0.9 %copy-done.4 = bf16[1,1,2,64,512]{4,3,2,1,0:T(8,128)(2,1)S(1)} copy-done((bf16[1,1,2,64,512]{4,3,2,1,0:T(8,128)(2,1)S(1)}, bf16[1,1,2,64,512]{4,3,2,1,0:T(8,128)(2,1)}, u32[]{:S(2)}) %copy-start.4) | copy-done | bytes 131096
  6.4 49.6 %attention_grads.1 = (bf16[128,2048]{1,0:T(8,128)(2,1)S(1)}, bf16[128,512]{1,0:T(8,128)(2,1)S(1)}, bf16[128,512]{1,0:T(8,128)(2,1)S(1)}, f32[64,1024]{1,0:T(8,128)S(1)}) custom-call(bf16[128,2048]{1,0:T(8,128)(2,1)S(1)} %bitcast.10, bf16[128,512]{1,0:T(8,128)(2,1)S(1)} %bitcast.14, bf16[128,512]{1,0:T(8,128)(2,1)S(1)} %bitcast.15, ...), custom_call_target="tpu_custom_call" | custom-call | tf_op jit(solution)/shard_map/attention_grads/pallas_call | solution.py:303
  56.0 0.8 %copy.14 = bf16[1,1,2,64,2048]{4,3,2,1,0:T(8,128)(2,1)} copy(bf16[1,1,2,64,2048]{4,3,2,1,0:T(8,128)(2,1)S(1)} %bitcast.12) | data formatting | bytes 1048576
  56.8 0.7 %copy.15 = bf16[1,1,2,64,512]{4,3,2,1,0:T(8,128)(2,1)} copy(bf16[1,1,2,64,512]{4,3,2,1,0:T(8,128)(2,1)S(1)} %bitcast.17) | data formatting | bytes 262144
  57.4 0.7 %copy.16 = bf16[1,1,2,64,512]{4,3,2,1,0:T(8,128)(2,1)} copy(bf16[1,1,2,64,512]{4,3,2,1,0:T(8,128)(2,1)S(1)} %bitcast.16) | data formatting | bytes 262144
  58.1 0.7 %copy.17 = f32[1024,64]{0,1:T(8,128)} copy(f32[1024,64]{0,1:T(8,128)S(1)} %bitcast.13) | data formatting | bytes 524288
Async XLA Ops:
  0.6 0.7 %copy-start.5 = (s32[1,16]{1,0:T(1,128)S(1)}, s32[1,16]{1,0:T(1,128)}, u32[]{:S(2)}) copy-start(s32[1,16]{1,0:T(1,128)} %len_ref.1) | copy-start | bytes 196
  1.3 1.2 %copy-start = (bf16[1,1,2,64,4096]{4,3,2,1,0:T(8,128)(2,1)S(1)}, bf16[1,1,2,64,4096]{4,3,2,1,0:T(8,128)(2,1)}, u32[]{:S(2)}) copy-start(bf16[1,1,2,64,4096]{4,3,2,1,0:T(8,128)(2,1)} %param.10) | copy-start | bytes 3145732
  2.5 1.0 %copy-start.1 = (bf16[1,1,2,64,2048]{4,3,2,1,0:T(8,128)(2,1)S(1)}, bf16[1,1,2,64,2048]{4,3,2,1,0:T(8,128)(2,1)}, u32[]{:S(2)}) copy-start(bf16[1,1,2,64,2048]{4,3,2,1,0:T(8,128)(2,1)} %param.6) | copy-start | bytes 1572868
  3.6 1.0 %copy-start.2 = (bf16[1,1,2,64,2048]{4,3,2,1,0:T(8,128)(2,1)S(1)}, bf16[1,1,2,64,2048]{4,3,2,1,0:T(8,128)(2,1)}, u32[]{:S(2)}) copy-start(bf16[1,1,2,64,2048]{4,3,2,1,0:T(8,128)(2,1)} %param.9) | copy-start | bytes 1572868
  4.6 0.9 %copy-start.3 = (bf16[1,1,2,64,512]{4,3,2,1,0:T(8,128)(2,1)S(1)}, bf16[1,1,2,64,512]{4,3,2,1,0:T(8,128)(2,1)}, u32[]{:S(2)}) copy-start(bf16[1,1,2,64,512]{4,3,2,1,0:T(8,128)(2,1)} %param.7) | copy-start | bytes 393220
  5.5 0.9 %copy-start.4 = (bf16[1,1,2,64,512]{4,3,2,1,0:T(8,128)(2,1)S(1)}, bf16[1,1,2,64,512]{4,3,2,1,0:T(8,128)(2,1)}, u32[]{:S(2)}) copy-start(bf16[1,1,2,64,512]{4,3,2,1,0:T(8,128)(2,1)} %param.8) | copy-start | bytes 393220
